TPU v7x, 256 devices: a whole 4x4x8 slice. The times are simulated.
256 devices in a mesh: freq: 8 (over z), tile: 32 (over y, x, core).
Axes of the slice: x: 4, y: 4, z: 8, core: 2. Of those that a mesh axis runs over, the one named last changes fastest.
Arguments:
- start_field: float32 [2, 8, 16384, 128], P(None, 'freq', 'tile'), may hold values from -6 to 6
- u_tiles: bfloat16 [2, 8, 32, 32, 64, 512], P(None, 'freq', 'tile'), may hold values from -0.09375 to 0.09375
- v_tiles: bfloat16 [2, 8, 32, 32, 64, 512], P(None, 'freq', None, 'tile'), may hold values from -0.1875 to 0.1875
- ranks: int32 [8, 32, 32], P('freq'), may hold values from 16 to 64, as said below
- onset_rec: int32 [32], P('tile'), may hold values from 8 to 24
- onset_src: int32 [32], P('tile'), may hold values from 8 to 24
Outputs:
- plus_field: float32 [2, 8, 16384, 128], P(None, 'freq', 'tile')
- minus_field: float32 [2, 8, 16384, 128], P(None, 'freq', 'tile')
Inputs may be any that keep to these rules, and one draw needn't show every extreme that they name: `ranks`: every rank is 16, 32 or 64, and 64 occurs at every frequency.
All inputs are finite; a program needn't handle non-finite values.
Results may differ from a plain program's by a relative error of at most 0.0065.
Values may be sent and summed in bfloat16 or wider, within the bound.
A program may use at most 64 MiB of HBM per device.

v0:
```python
import math

import jax
import jax.numpy as jnp
from jax import lax
from jax.sharding import PartitionSpec as P

ITERS = 2


def window_matrix(onset, count_freq):
    total_time = 4 * count_freq
    times = jnp.arange(total_time, dtype=jnp.float32)
    omegas = (jnp.arange(count_freq, dtype=jnp.float32) + 1.0) * (2.0 * math.pi / total_time)
    phase = omegas[:, None] * times[None, :]
    stacked = jnp.concatenate([jnp.cos(phase), -jnp.sin(phase)], 0)
    kept_times = (jnp.arange(total_time, dtype=jnp.int32) < onset).astype(jnp.float32)
    return jnp.dot(
        stacked * kept_times[None, :], 2.0 / total_time * stacked.T, precision=lax.Precision.HIGHEST
    )


def time_window(field, onset):
    local_count = field.shape[1]
    freq_count = lax.axis_size("freq") * local_count
    matrix = window_matrix(onset, freq_count)
    first_freq = lax.axis_index("freq") * local_count
    quarters = matrix.reshape(2, freq_count, 2, freq_count)
    own_rows = lax.dynamic_slice_in_dim(quarters, first_freq, local_count, 1)
    return jnp.einsum(
        "afbk,bknp->afnp",
        own_rows,
        lax.all_gather(field, "freq", axis=1, tiled=True),
        precision=lax.Precision.HIGHEST,
    )


def slot_mask(rank_block, slot_count):
    slots = jnp.arange(slot_count, dtype=jnp.int32)
    masked = (slots[None, None, :] < rank_block[:, :, None]).astype(jnp.float32)
    return jnp.transpose(masked, (1, 0, 2))[..., None]


def forward_apply(current, u_tiles, v_tiles, ranks):
    column = lax.axis_index("tile")
    source_b = current.astype(jnp.bfloat16)
    v_real, v_imag = (v_tiles[0, :, :, 0], v_tiles[1, :, :, 0])
    pattern = "fisn,fnp->ifsp"
    real_w = jnp.einsum(
        pattern, v_real, source_b[0], preferred_element_type=jnp.float32
    ) - jnp.einsum(pattern, v_imag, source_b[1], preferred_element_type=jnp.float32)
    imag_w = jnp.einsum(
        pattern, v_real, source_b[1], preferred_element_type=jnp.float32
    ) + jnp.einsum(pattern, v_imag, source_b[0], preferred_element_type=jnp.float32)
    column_ranks = lax.dynamic_index_in_dim(ranks, column, 2, keepdims=False)
    masked = slot_mask(column_ranks, v_real.shape[2])
    sending = jnp.stack([real_w * masked, imag_w * masked], 1).astype(jnp.bfloat16)
    arrived = lax.all_to_all(sending, "tile", split_axis=0, concat_axis=0, tiled=True)
    u_real, u_imag = (u_tiles[0, :, 0], u_tiles[1, :, 0])
    pattern = "fjsm,jfsp->fmp"
    real_y = jnp.einsum(
        pattern, u_real, arrived[:, 0], preferred_element_type=jnp.float32
    ) - jnp.einsum(pattern, u_imag, arrived[:, 1], preferred_element_type=jnp.float32)
    imag_y = jnp.einsum(
        pattern, u_real, arrived[:, 1], preferred_element_type=jnp.float32
    ) + jnp.einsum(pattern, u_imag, arrived[:, 0], preferred_element_type=jnp.float32)
    return jnp.stack([real_y, imag_y], 0)


def adjoint_apply(minus_b, u_tiles, v_tiles, ranks):
    row_index = lax.axis_index("tile")
    u_real, u_imag = (u_tiles[0, :, 0], u_tiles[1, :, 0])
    pattern = "fjsm,fmp->jfsp"
    real_q = jnp.einsum(
        pattern, u_real, minus_b[0], preferred_element_type=jnp.float32
    ) + jnp.einsum(pattern, u_imag, minus_b[1], preferred_element_type=jnp.float32)
    imag_q = jnp.einsum(
        pattern, u_real, minus_b[1], preferred_element_type=jnp.float32
    ) - jnp.einsum(pattern, u_imag, minus_b[0], preferred_element_type=jnp.float32)
    row_ranks = lax.dynamic_index_in_dim(ranks, row_index, 1, keepdims=False)
    masked = slot_mask(row_ranks, u_real.shape[2])
    sending = jnp.stack([real_q * masked, imag_q * masked], 1).astype(jnp.bfloat16)
    arrived = lax.all_to_all(sending, "tile", split_axis=0, concat_axis=0, tiled=True)
    v_real, v_imag = (v_tiles[0, :, :, 0], v_tiles[1, :, :, 0])
    pattern = "fisn,ifsp->fnp"
    real_p = jnp.einsum(
        pattern, v_real, arrived[:, 0], preferred_element_type=jnp.float32
    ) + jnp.einsum(pattern, v_imag, arrived[:, 1], preferred_element_type=jnp.float32)
    imag_p = jnp.einsum(
        pattern, v_real, arrived[:, 1], preferred_element_type=jnp.float32
    ) - jnp.einsum(pattern, v_imag, arrived[:, 0], preferred_element_type=jnp.float32)
    return jnp.stack([real_p, imag_p], 0)


def on_device(start_field, u_tiles, v_tiles, ranks, onset_rec, onset_src):
    current = start_field
    minus_field = None
    for sweep_index in range(ITERS):
        image = forward_apply(current, u_tiles, v_tiles, ranks)
        minus_field = time_window(image, onset_rec[0])
        back = adjoint_apply(minus_field.astype(jnp.bfloat16), u_tiles, v_tiles, ranks)
        current = start_field + time_window(back, onset_src[0])
    return (current, minus_field)


def solution(mesh):
    in_specs = (
        P(None, "freq", "tile", None),
        P(None, "freq", "tile", None, None, None),
        P(None, "freq", None, "tile", None, None),
        P("freq", None, None),
        P("tile"),
        P("tile"),
    )
    out_specs = (P(None, "freq", "tile", None), P(None, "freq", "tile", None))
    return jax.shard_map(
        on_device, mesh=mesh, in_specs=in_specs, out_specs=out_specs, check_vma=False
    )
```

profile of v0, /device:TPU:8, one launch (start us, length us, event | category | flops | bytes accessed | tf_op | source)
XLA Modules:
  0.0 391.6 jit_solution(15126953091048446742)
XLA Ops:
  7.2 1.1 convert_element_type.88
  8.3 2.3 fusion.170
  10.6 2.3 fusion.171
  13.2 2.3 fusion.93
  15.5 2.5 fusion.92
  18.2 22.3 %all_to_all.20 = bf16[32,2,1,64,128]{4,3,2,1,0:T(8,128)(2,1)S(1)} all-to-all(bf16[32,2,1,64,128]{4,3,2,1,0:T(8,128)(2,1)S(1)} %copy.44), channel_id=1, replica_groups=mesh['freq'=8,'tile'=32] {'tile'}, dimensions={0} | all-to-all | bytes 2097152 | tf_op jit(solution)/shard_map/all_to_all | solution.py:58
  42.3 0.8 pad_maximum_fusion.4
  44.3 55.2 %all-gather.5.cloned.1.call-done = f32[2,8,512,128]{2,3,1,0:T(8,128)} async-done(((f32[2,1,512,128]{2,3,1,0:T(8,128)}), f32[2,8,512,128]{2,3,1,0:T(8,128)}) %all-gather.5.cloned.1.call-update) | async-done | bytes 4194320 | tf_op jit(solution)/shard_map/all_gather | solution.py:33
  99.6 5.5 %copy.48 = f32[2,8,512,128]{3,1,0,2:T(8,128)} copy(f32[2,8,512,128]{2,3,1,0:T(8,128)} %all-gather.5.cloned.1.call-done) | data formatting | bytes 8388608 | tf_op jit(solution)/shard_map/all_gather | solution.py:33
  105.1 5.0 %fusion.111 = bf16[2,512,128]{2,0,1:T(2,128)(2,1)S(1)} fusion(f32[2,8,512,128]{3,1,0,2:T(8,128)} %copy.48, f32[2,2,8]{2,1,0:T(2,128)S(1)} %dynamic-slice_bitcast_fusion), kind=kOutput, calls=%fused_computation.80 | convolution fusion | flops 25296896 | bytes 4456576 | tf_op jit(solution)/shard_map/afbk,bknp->afnp/dot_general | solution.py:30
  111.9 0.7 fusion.105
  112.7 0.7 fusion.102
  113.6 22.3 %all_to_all.21 = bf16[32,2,1,64,128]{4,3,2,1,0:T(8,128)(2,1)S(1)} all-to-all(bf16[32,2,1,64,128]{4,3,2,1,0:T(8,128)(2,1)S(1)} %copy.49), channel_id=1, replica_groups=mesh['freq'=8,'tile'=32] {'tile'}, dimensions={0} | all-to-all | bytes 2097152 | tf_op jit(solution)/shard_map/all_to_all | solution.py:83
  137.7 0.8 pad_maximum_fusion.5
  139.5 51.3 %all-gather.7.cloned.1.call-done = f32[2,8,512,128]{2,3,1,0:T(8,128)} async-done(((f32[2,1,512,128]{2,3,1,0:T(8,128)}), f32[2,8,512,128]{2,3,1,0:T(8,128)}) %all-gather.7.cloned.1.call-update) | async-done | bytes 4194320 | tf_op jit(solution)/shard_map/all_gather | solution.py:33
  190.9 5.5 %copy.53 = f32[2,8,512,128]{3,1,0,2:T(8,128)} copy(f32[2,8,512,128]{2,3,1,0:T(8,128)} %all-gather.7.cloned.1.call-done) | data formatting | bytes 8388608 | tf_op jit(solution)/shard_map/all_gather | solution.py:33
  196.4 5.3 %fusion.110 = bf16[2,1,512,128]{3,0,2,1:T(2,128)(2,1)S(1)} fusion(f32[2,8,512,128]{3,1,0,2:T(8,128)} %copy.53, f32[2,1,512,128]{3,2,1,0:T(8,128)S(1)} %copy-done.9, f32[2,2,8]{2,1,0:T(2,128)S(1)} %dynamic-slice_bitcast_fusion.1), kind=kOutput, calls=%fused_computation.79 | convolution fusion | flops 25427968 | bytes 4980864 | tf_op jit(solution)/shard_map/afbk,bknp->afnp/dot_general | solution.py:30
  203.5 0.7 fusion.94
  205.2 22.2 %all_to_all.22 = bf16[32,2,1,64,128]{4,3,2,1,0:T(8,128)(2,1)S(1)} all-to-all(bf16[32,2,1,64,128]{4,3,2,1,0:T(8,128)(2,1)S(1)} %copy.55), channel_id=1, replica_groups=mesh['freq'=8,'tile'=32] {'tile'}, dimensions={0} | all-to-all | bytes 2097152 | tf_op jit(solution)/shard_map/all_to_all | solution.py:58
  229.3 0.8 pad_maximum_fusion.6
  230.4 51.9 %all-gather.9.cloned.1.call-done = f32[2,8,512,128]{2,3,1,0:T(8,128)} async-done(((f32[2,1,512,128]{2,3,1,0:T(8,128)}), f32[2,8,512,128]{2,3,1,0:T(8,128)}) %all-gather.9.cloned.1.call-update) | async-done | bytes 4194320 | tf_op jit(solution)/shard_map/all_gather | solution.py:33
  282.4 5.5 %copy.59 = f32[2,8,512,128]{3,1,0,2:T(8,128)} copy(f32[2,8,512,128]{2,3,1,0:T(8,128)} %all-gather.9.cloned.1.call-done) | data formatting | bytes 8388608 | tf_op jit(solution)/shard_map/all_gather | solution.py:33
  287.9 5.0 %bitcast_convert_fusion = (bf16[2,512,128]{2,0,1:T(2,128)(2,1)S(1)}, f32[2,512,128,1]{2,0,3,1:T(2,128)S(1)}) fusion(f32[2,8,512,128]{3,1,0,2:T(8,128)} %copy.59, f32[2,2,8]{2,1,0:T(2,128)S(1)} %dynamic-slice_bitcast_fusion), kind=kOutput, calls=%fused_computation.129 | convolution fusion | flops 25296896 | bytes 4980864 | tf_op jit(solution)/shard_map/afbk,bknp->afnp/dot_general | solution.py:30
  294.8 0.7 fusion.99
  295.5 0.7 fusion.96
  296.4 22.2 %all_to_all.23 = bf16[32,2,1,64,128]{4,3,2,1,0:T(8,128)(2,1)S(1)} all-to-all(bf16[32,2,1,64,128]{4,3,2,1,0:T(8,128)(2,1)S(1)} %copy.60), channel_id=1, replica_groups=mesh['freq'=8,'tile'=32] {'tile'}, dimensions={0} | all-to-all | bytes 2097152 | tf_op jit(solution)/shard_map/all_to_all | solution.py:83
  320.6 0.8 pad_maximum_fusion.7
  321.4 0.8 copy.67
  322.3 51.4 %all-gather.11.cloned.1.call-done = f32[2,8,512,128]{2,3,1,0:T(8,128)} async-done(((f32[2,1,512,128]{2,3,1,0:T(8,128)}), f32[2,8,512,128]{2,3,1,0:T(8,128)}) %all-gather.11.cloned.1.call-update) | async-done | bytes 4194320 | tf_op jit(solution)/shard_map/all_gather | solution.py:33
  373.7 5.5 %copy.64 = f32[2,8,512,128]{3,1,0,2:T(8,128)} copy(f32[2,8,512,128]{2,3,1,0:T(8,128)} %all-gather.11.cloned.1.call-done) | data formatting | bytes 8388608 | tf_op jit(solution)/shard_map/all_gather | solution.py:33
  379.2 5.1 %fusion.108 = f32[2,1,512,128]{3,0,2,1:T(2,128)S(1)} fusion(f32[2,8,512,128]{3,1,0,2:T(8,128)} %copy.64, f32[2,1,512,128]{3,2,1,0:T(8,128)S(1)} %copy-done.9, f32[2,2,8]{2,1,0:T(2,128)S(1)} %dynamic-slice_bitcast_fusion.1), kind=kOutput, calls=%fused_computation.75 | convolution fusion | flops 25296896 | bytes 5243008 | tf_op jit(solution)/shard_map/afbk,bknp->afnp/dot_general | solution.py:30
  384.3 0.8 copy.66
  (76 shorter events, 15.8 us)
Async XLA Ops:
  7.2 5.7 %copy-start = (s32[1,32,32]{2,1,0:T(8,128)S(1)}, s32[1,32,32]{2,1,0:T(8,128)}, u32[]{:S(2)}) copy-start(s32[1,32,32]{2,1,0:T(8,128)} %param.9) | copy-start | bytes 12292
  7.2 92.4 %all-gather.5.cloned.1.call-start = ((), (), s32[]{:S(2)}) async-start(), calls=%async_computation.4 | async-start | bytes 4718592 | tf_op jit(solution)/shard_map/all_gather | solution.py:33
  15.5 24.9 %copy-start.2 = (bf16[2,1,1,32,64,512]{5,4,3,2,1,0:T(8,128)(2,1)S(1)}, bf16[2,1,1,32,64,512]{5,4,3,2,1,0:T(8,128)(2,1)}, u32[]{:S(2)}) copy-start(bf16[2,1,1,32,64,512]{5,4,3,2,1,0:T(8,128)(2,1)} %param.7) | copy-start | bytes 12582916
  43.2 147.7 %all-gather.7.cloned.1.call-start = ((), (), s32[]{:S(2)}) async-start(), calls=%async_computation.5 | async-start | bytes 4718592 | tf_op jit(solution)/shard_map/all_gather | solution.py:33
  105.1 5.4 %copy-start.3 = (bf16[2,1,1,32,64,512]{5,4,3,2,1,0:T(8,128)(2,1)S(1)}, bf16[2,1,1,32,64,512]{5,4,3,2,1,0:T(8,128)(2,1)}, u32[]{:S(2)}) copy-start(bf16[2,1,1,32,64,512]{5,4,3,2,1,0:T(8,128)(2,1)} %param.7) | copy-start | bytes 12582916
  112.6 23.2 %copy-start.6 = (bf16[2,1,32,1,64,512]{5,4,3,2,1,0:T(8,128)(2,1)S(1)}, bf16[2,1,32,1,64,512]{5,4,3,2,1,0:T(8,128)(2,1)}, u32[]{:S(2)}) copy-start(bf16[2,1,32,1,64,512]{5,4,3,2,1,0:T(8,128)(2,1)} %param.8) | copy-start | bytes 12582916
  138.6 143.8 %all-gather.9.cloned.1.call-start = ((), (), s32[]{:S(2)}) async-start(), calls=%async_computation.6 | async-start | bytes 4718592 | tf_op jit(solution)/shard_map/all_gather | solution.py:33
  139.5 56.9 %copy-start.9 = (f32[2,1,512,128]{3,2,1,0:T(8,128)S(1)}, f32[2,1,512,128]{3,2,1,0:T(8,128)}, u32[]{:S(2)}) copy-start(f32[2,1,512,128]{3,2,1,0:T(8,128)} %param.6) | copy-start | bytes 1572868
  196.4 5.7 %copy-start.7 = (bf16[2,1,32,1,64,512]{5,4,3,2,1,0:T(8,128)(2,1)S(1)}, bf16[2,1,32,1,64,512]{5,4,3,2,1,0:T(8,128)(2,1)}, u32[]{:S(2)}) copy-start(bf16[2,1,32,1,64,512]{5,4,3,2,1,0:T(8,128)(2,1)} %param.8) | copy-start | bytes 12582916
  204.2 23.2 %copy-start.4 = (bf16[2,1,1,32,64,512]{5,4,3,2,1,0:T(8,128)(2,1)S(1)}, bf16[2,1,1,32,64,512]{5,4,3,2,1,0:T(8,128)(2,1)}, u32[]{:S(2)}) copy-start(bf16[2,1,1,32,64,512]{5,4,3,2,1,0:T(8,128)(2,1)} %param.7) | copy-start | bytes 12582916
  230.2 143.5 %all-gather.11.cloned.1.call-start = ((), (), s32[]{:S(2)}) async-start(), calls=%async_computation.7 | async-start | bytes 4718592 | tf_op jit(solution)/shard_map/all_gather | solution.py:33
  287.9 5.4 %copy-start.5 = (bf16[2,1,1,32,64,512]{5,4,3,2,1,0:T(8,128)(2,1)S(1)}, bf16[2,1,1,32,64,512]{5,4,3,2,1,0:T(8,128)(2,1)}, u32[]{:S(2)}) copy-start(bf16[2,1,1,32,64,512]{5,4,3,2,1,0:T(8,128)(2,1)} %param.7) | copy-start | bytes 12582916
  295.5 23.2 %copy-start.8 = (bf16[2,1,32,1,64,512]{5,4,3,2,1,0:T(8,128)(2,1)S(1)}, bf16[2,1,32,1,64,512]{5,4,3,2,1,0:T(8,128)(2,1)}, u32[]{:S(2)}) copy-start(bf16[2,1,32,1,64,512]{5,4,3,2,1,0:T(8,128)(2,1)} %param.8) | copy-start | bytes 12582916
  373.7 11.4 %copy-start.1 = (s32[1,32,32]{2,1,0:T(8,128)S(1)}, s32[1,32,32]{2,1,0:T(8,128)}, u32[]{:S(2)}) copy-start(s32[1,32,32]{2,1,0:T(8,128)} %param.9) | copy-start | bytes 12292
Sparse Core Ops, SparseCore 0:
  43.3 56.2 all-gather.4
  138.7 52.1 all-gather.6
  230.3 52.0 all-gather.8
  321.6 52.0 all-gather.10
where the time goes:
time: 393 us; the launch traced here: 392 us
  waiting for transfers between devices  210 us (53%)
  blocking collectives  89 us (23%)
  matrix products  46.1 us (12%)
  local copies, waits for them, and re-layouts  25.6 us (7%)
  between operations  15.5 us (4%)
  other arithmetic  5.07 us (1%)
    all_gather x4, waiting for transfers between devices, time_window(): lax.all_gather(field, 'freq', axis=1, tiled=True)  210 us
    all_to_all x2, blocking collectives, forward_apply(): lax.all_to_all(sending, 'tile', split_axis=0, concat_axis=0, tiled=True)  44.5 us
    all_to_all x2, blocking collectives, adjoint_apply(): lax.all_to_all(sending, 'tile', split_axis=0, concat_axis=0, tiled=True)  44.5 us
    all_gather x4, local copies, waits for them, and re-layouts, time_window(): lax.all_gather(field, 'freq', axis=1, tiled=True)  22.1 us
    dot_general x4, matrix products, time_window(): jnp.einsum('afbk,bknp->afnp', own_rows, lax.all_gather(field, 'freq', axi...  20.4 us
  transfers between devices with their start and end apart: 4, of which 4 were waited for; matrix products, arithmetic and copies ran while one was open for 0% of the time, Pallas kernels for 0%

commit v1 on v0

v1 whole, which is shorter than its diff:
```python
import functools
import math

import jax
import jax.numpy as jnp
import numpy as np
from jax import lax
from jax.experimental import pallas as pl
from jax.experimental.pallas import tpu as pltpu
from jax.sharding import PartitionSpec as P

ITERS = 2
STEPS = 2 * ITERS
CHAINS = 2
NY, NX, NC = 4, 4, 2
NT = NY * NX * NC
NF = 8
GROUP = NX * NC
SLOTS = 64
GS = GROUP * SLOTS
POS = 512
POINTS = 128
ROWS = 2 * POINTS // CHAINS
CHUNK = ROWS // NF
PC = CHUNK // 2
TIMES = 4 * NF
MESH = pl.DeviceIdType.MESH
BF = jnp.bfloat16
F32 = jnp.float32
Y_ORDER = (2, 1, 3, 0)
X_ORDER = (2, 1, 3, 0)
Z_ORDER = (4, 3, 5, 2, 6, 1, 7)


def dot(a, b):
    return jnp.dot(a, b, preferred_element_type=F32)


def phase_rows():
    times = np.arange(TIMES, dtype=np.float64)
    omegas = (np.arange(NF, dtype=np.float64) + 1.0) * (2.0 * math.pi / TIMES)
    phase = omegas[:, None] * times[None, :]
    both = np.stack([np.cos(phase), -np.sin(phase)], 1)
    return np.repeat(both.reshape(2 * NF, TIMES), PC, axis=0).astype(np.float32)


def combine(first, second, sign):
    first = first.reshape(NF, 2, PC, first.shape[-1])
    second = second.reshape(NF, 2, PC, second.shape[-1]) * sign
    real = first[:, 0] - second[:, 1]
    imag = first[:, 1] + second[:, 0]
    return jnp.stack([real, imag], 1).reshape(ROWS, first.shape[-1])


def kernel(
    ranks, onset_rec, onset_src, phases, phases_t, start, u_hbm, v_hbm, plus_out, minus_out,
    nat, tr, st, w_send, w_recv, z1_send, z1_recv, z2_send, z2_recv, mask, window,
    load_sem, ws_sem, wr_sem, z1s_sem, z1r_sem, z2s_sem, z2r_sem,
):
    f = lax.axis_index("freq")
    me = lax.axis_index("tile")
    y, x, c = me // GROUP, (me // NC) % NX, me % NC

    def tile_of(dy, dx, dc):
        return ((y + dy) % NY) * GROUP + ((x + dx) % NX) * NC + (c + dc) % NC

    barrier = pltpu.get_barrier_semaphore()
    def load(which, group):
        source = v_hbm if which == 1 else u_hbm
        return pltpu.make_async_copy(source.at[:, group], nat.at[which, :, group], load_sem.at[which, group])

    for which in (1, 0):
        for group in range(NY):
            load(which, group).start()
    for dy in range(NY):
        for dx in range(NX):
            for dc in range(NC):
                if (dy, dx, dc) != (0, 0, 0):
                    pl.semaphore_signal(barrier, inc=1, device_id=(f, tile_of(dy, dx, dc)), device_id_type=MESH)
    for dz in range(1, NF):
        pl.semaphore_signal(barrier, inc=1, device_id=((f + dz) % NF, me), device_id_type=MESH)

    for part in range(2):
        turned = start[part].T
        for h in range(CHAINS):
            for k in range(NF):
                p0 = h * (POINTS // CHAINS) + k * PC
                r0 = k * CHUNK + part * PC
                st[h, r0 : r0 + PC, :] = turned[p0 : p0 + PC, :]
    for h in range(CHAINS):
        z2_recv[0, h] = jnp.zeros((NF, CHUNK, POS), BF)

    lanes = lax.broadcasted_iota(jnp.int32, (1, 2 * SLOTS), 1)
    for pair in range(NT // 2):
        group, l0 = pair // (GROUP // 2), pair % (GROUP // 2) * 2 * SLOTS
        for adj in range(2):
            low = ranks[2 * pair, me] if adj == 0 else ranks[me, 2 * pair]
            high = ranks[2 * pair + 1, me] if adj == 0 else ranks[me, 2 * pair + 1]
            bound = jnp.where(lanes < SLOTS, low, high + SLOTS)
            mask[adj, group, :, l0 : l0 + 2 * SLOTS] = jnp.where(lanes < bound, 1.0, 0.0).astype(F32)

    for group in range(NY):
        load(1, group).wait()
        for part in range(2):
            tr[0, part, group] = nat[1, part, group].T

    pl.semaphore_wait(barrier, NT - 1 + NF - 1)

    def setup_late():
        for adj, onset in ((0, onset_rec), (1, onset_src)):
            ticks = lax.broadcasted_iota(jnp.int32, (1, TIMES), 1)
            kept = jnp.where(ticks < onset[0], 1.0, 0.0).astype(F32)
            full = jnp.dot(phases[...] * kept, phases_t[...], precision=lax.Precision.HIGHEST, preferred_element_type=F32)
            r = lax.broadcasted_iota(jnp.int32, (ROWS, ROWS), 0)
            q = lax.broadcasted_iota(jnp.int32, (ROWS, ROWS), 1)
            full = jnp.where(r % PC == q % PC, full, 0.0)
            high = full.astype(BF)
            rest = full - high.astype(F32)
            middle = rest.astype(BF)
            low = (rest - middle.astype(F32)).astype(BF)
            window[adj, 0] = high
            window[adj, 1] = middle
            window[adj, 2] = low
        for group in range(NY):
            load(0, group).wait()
            for part in range(2):
                tr[1, part, group] = nat[0, part, group].T

    def coefficients(t, h, adj, sign):
        even = (1 - adj).astype(F32)

        @pl.when(t > 0)
        def _():
            z_wait(z2_recv.at[t, h], z2r_sem.at[t - 1, h])

        field = (st[h] * even + z2_recv[t, h].reshape(ROWS, POS).astype(F32)).astype(BF)
        for dy in Y_ORDER:
            group = (y + dy) % NY
            w = combine(dot(field, tr[adj, 0, group]), dot(field, tr[adj, 1, group]), sign)
            w = (w * mask[adj, group]).astype(BF)
            w_send[t, h, group] = w.T
            for dx in X_ORDER:
                for dc in (1, 0):
                    to = ((x + dx) % NX) * NC + (c + dc) % NC
                    chunk = w_send.at[t, h, group, pl.ds(to * SLOTS, SLOTS)]
                    mine = pl.ds((me % GROUP) * SLOTS, SLOTS)
                    if (dy, dx, dc) == (0, 0, 0):
                        w_recv[t, h, y, mine] = w_send[t, h, group, pl.ds(to * SLOTS, SLOTS)]
                        continue
                    pltpu.make_async_remote_copy(
                        src_ref=chunk, dst_ref=w_recv.at[t, h, y, mine],
                        send_sem=ws_sem.at[t, h], recv_sem=wr_sem.at[t, h, dy],
                        device_id=(f, group * GROUP + to), device_id_type=MESH,
                    ).start()

    def z_wait(buffer, semaphore):
        part = buffer.at[pl.ds(0, NF - 1)]
        pltpu.make_async_copy(part, part, semaphore).wait()

    def z_send(source, target, send_sem, recv_sem):
        for dz in Z_ORDER:
            to = (f + dz) % NF
            pltpu.make_async_remote_copy(
                src_ref=source.at[to], dst_ref=target.at[f], send_sem=send_sem, recv_sem=recv_sem,
                device_id=(to, me), device_id_type=MESH,
            ).start()

    def apply(t, h, adj, sign):
        real = imag = None
        for dy in Y_ORDER:
            group = (y - dy + NY) % NY
            count = GS - SLOTS if dy == 0 else GS
            part = w_recv.at[t, h, group, pl.ds(0, count)]
            pltpu.make_async_copy(part, part, wr_sem.at[t, h, dy]).wait()
            w = w_recv[t, h, group].T
            one, two = dot(w, nat[adj, 0, group]), dot(w, nat[adj, 1, group])
            real, imag = (one, two) if real is None else (real + one, imag + two)
        image = combine(real, imag, sign).astype(BF)
        z1_send[t, h] = image.reshape(NF, CHUNK, POS)
        z1_recv[t, h, f] = z1_send[t, h, f]
        z_send(z1_send.at[t, h], z1_recv.at[t, h], z1s_sem.at[t, h], z1r_sem.at[t, h])

    def windowed(t, h, adj):
        z_wait(z1_recv.at[t, h], z1r_sem.at[t, h])
        traces = z1_recv[t, h].reshape(ROWS, POS)
        out = dot(window[adj, 2], traces) + dot(window[adj, 1], traces) + dot(window[adj, 0], traces)
        z2_send[t, h] = out.astype(BF).reshape(NF, CHUNK, POS)
        z2_recv[t + 1, h, f] = z2_send[t, h, f]
        z_send(z2_send.at[t, h], z2_recv.at[t + 1, h], z2s_sem.at[t, h], z2r_sem.at[t, h])

    def turn_out(t, out, with_start):
        for part in range(2):
            rows = []
            for h in range(CHAINS):
                values = z2_recv[t, h].astype(F32).reshape(ROWS, POS)
                if with_start:
                    values = st[h] + values
                rows.append(values.reshape(NF, 2, PC, POS)[:, part].reshape(ROWS // 2, POS))
            out[part] = jnp.concatenate(rows, 0).T

    def body(t, carry):
        adj = t % 2
        sign = (1 - 2 * adj).astype(F32)
        for h in range(CHAINS):
            coefficients(t, h, adj, sign)
        pl.when(t == 0)(setup_late)
        pl.when(t == STEPS - 1)(lambda: turn_out(STEPS - 1, minus_out, False))
        for h in range(CHAINS):
            apply(t, h, adj, sign)
        for h in range(CHAINS):
            windowed(t, h, adj)
        return carry

    lax.fori_loop(0, STEPS, body, 0)
    for h in range(CHAINS):
        z_wait(z2_recv.at[STEPS, h], z2r_sem.at[STEPS - 1, h])
    turn_out(STEPS, plus_out, True)

    def drain(t, carry):
        for h in range(CHAINS):
            part = w_send.at[t, h, pl.ds(0, NY), pl.ds(0, GS)]
            for group in range(NY):
                count = GS - SLOTS if group == 0 else GS
                part = w_send.at[t, h, group, pl.ds(0, count)]
                pltpu.make_async_copy(part, part, ws_sem.at[t, h]).wait()
            z_wait(z1_send.at[t, h], z1s_sem.at[t, h])
            z_wait(z2_send.at[t, h], z2s_sem.at[t, h])
        return carry

    lax.fori_loop(0, STEPS, drain, 0)


def on_device(start_field, u_tiles, v_tiles, ranks, onset_rec, onset_src):
    rows = phase_rows()
    smem = pl.BlockSpec(memory_space=pltpu.SMEM)
    vmem = pl.BlockSpec(memory_space=pltpu.VMEM)
    hbm = pl.BlockSpec(memory_space=pl.ANY)
    field = jax.ShapeDtypeStruct((2, POS, POINTS), F32)
    plus, minus = pl.pallas_call(
        kernel,
        out_shape=(field, field),
        in_specs=[smem, smem, smem, vmem, vmem, vmem, hbm, hbm],
        out_specs=(vmem, vmem),
        scratch_shapes=[
            pltpu.VMEM((2, 2, NY, GS, POS), BF),
            pltpu.VMEM((2, 2, NY, POS, GS), BF),
            pltpu.VMEM((CHAINS, ROWS, POS), F32),
            pltpu.VMEM((STEPS, CHAINS, NY, GS, ROWS), BF),
            pltpu.VMEM((STEPS, CHAINS, NY, GS, ROWS), BF),
            pltpu.VMEM((STEPS, CHAINS, NF, CHUNK, POS), BF),
            pltpu.VMEM((STEPS, CHAINS, NF, CHUNK, POS), BF),
            pltpu.VMEM((STEPS, CHAINS, NF, CHUNK, POS), BF),
            pltpu.VMEM((STEPS + 1, CHAINS, NF, CHUNK, POS), BF),
            pltpu.VMEM((2, NY, 1, GS), F32),
            pltpu.VMEM((2, 3, ROWS, ROWS), BF),
            pltpu.SemaphoreType.DMA((2, NY)),
            pltpu.SemaphoreType.DMA((STEPS, CHAINS)),
            pltpu.SemaphoreType.DMA((STEPS, CHAINS, NY)),
            pltpu.SemaphoreType.DMA((STEPS, CHAINS)),
            pltpu.SemaphoreType.DMA((STEPS, CHAINS)),
            pltpu.SemaphoreType.DMA((STEPS, CHAINS)),
            pltpu.SemaphoreType.DMA((STEPS, CHAINS)),
        ],
        compiler_params=pltpu.CompilerParams(
            collective_id=0, has_side_effects=True, vmem_limit_bytes=52 * 2**20
        ),
        name="marchenko",
    )(
        ranks.reshape(NT, NT),
        onset_rec,
        onset_src,
        jnp.asarray(rows),
        jnp.asarray(2.0 / TIMES * rows.T),
        start_field.reshape(2, POS, POINTS),
        u_tiles.reshape(2, NY, GS, POS),
        v_tiles.reshape(2, NY, GS, POS),
    )
    shape = (2, 1, POS, POINTS)
    return plus.reshape(shape), minus.reshape(shape)


def solution(mesh):
    in_specs = (
        P(None, "freq", "tile", None),
        P(None, "freq", "tile", None, None, None),
        P(None, "freq", None, "tile", None, None),
        P("freq", None, None),
        P("tile"),
        P("tile"),
    )
    out_specs = (P(None, "freq", "tile", None), P(None, "freq", "tile", None))
    return jax.shard_map(
        on_device, mesh=mesh, in_specs=in_specs, out_specs=out_specs, check_vma=False
    )
```

time: 393 us -> 114 us (0.29)
  waiting for transfers between devices: 210 us -> 0 us
  Pallas kernels: 0 us -> 107 us
  blocking collectives: 89 us -> 0 us
  matrix products: 46.1 us -> 0 us
  local copies, waits for them, and re-layouts: 25.6 us -> 4.9 us
  between operations: 15.5 us -> 1.94 us
  other arithmetic: 5.07 us -> 0 us
    all_gather x4 -> x0, waiting for transfers between devices: 210 us -> none  [time_window(): lax.all_gather(field, 'freq', axis=1, tiled=True)]
    pallas_call x0 -> x1, Pallas kernels: none -> 107 us  [on_device(): pl.pallas_call(kernel, out_shape=(field, field), in_specs=[smem, smem, sm...]
    all_to_all x4 -> x0, blocking collectives: 89 us -> none  [the longest x2 44.5 us: forward_apply(): lax.all_to_all(sending, 'tile', split_axis=0, concat_axis=0, tiled=True)]
    dot_general x38 -> x0, matrix products: 46.1 us -> none  [the longest x4 20.4 us: time_window(): jnp.einsum('afbk,bknp->afnp', own_rows, lax.all_gather(field, 'freq', axi...]
    all_gather x4 -> x0, local copies, waits for them, and re-layouts: 22.1 us -> none  [time_window(): lax.all_gather(field, 'freq', axis=1, tiled=True)]
  transfers between devices with their start and end apart: 4 -> 0, of which waited for: 4 -> 0; matrix products, arithmetic and copies ran while one was open for 0% -> 0% of each run, Pallas kernels for 0% -> 0%
where the time goes in v1:
time: 114 us; the launch traced here: 113 us
  Pallas kernels  107 us (94%)
  local copies, waits for them, and re-layouts  4.9 us (4%)
  between operations  1.94 us (2%)
    pallas_call x1, Pallas kernels, on_device(): pl.pallas_call(kernel, out_shape=(field, field), in_specs=[smem, smem, sm...  107 us
    unnamed x10, local copies, waits for them, and re-layouts  4.9 us

profile of v1, /device:TPU:8, one launch (start us, length us, event | category | flops | bytes accessed | tf_op | source)
XLA Modules:
  0.0 113.3 jit_solution(7225919128383878112)
XLA Ops:
  1.9 0.0 copy-start
  1.9 1.0 copy-done
  3.0 0.0 copy-start.1
  3.0 0.8 copy-done.1
  3.8 0.0 copy-start.2
  3.8 0.7 copy-done.2
  4.5 0.0 copy-start.3
  4.5 0.7 copy-done.3
  5.2 106.5 %marchenko.1 = (f32[2,512,128]{2,1,0:T(8,128)S(1)}, f32[2,512,128]{2,1,0:T(8,128)S(1)}) custom-call(s32[32,32]{1,0:T(8,128)S(1)} %bitcast.13, s32[1]{0:T(128)S(6)} %copy.14.onset_rec, s32[1]{0:T(128)S(6)} %copy.15.onset_src, f32[128,32]{1,0:T(8,128)S(1)} %copy-done.1, f32[32,128]{1,0:T(8,128)S(1)} %copy-done.3, f32[2,512,128]{2,1,0:T(8,128)S(1)} %bitcast.10, ...), custom_call_target="tpu_custom_call" | custom-call | tf_op jit(solution)/shard_map/marchenko/pallas_call | solution.py:239
  111.8 0.8 copy.16
  112.6 0.8 copy.17
Async XLA Ops:
  1.9 1.0 copy-start
  3.0 0.8 copy-start.1
  3.8 0.7 copy-start.2
  4.5 0.7 copy-start.3

commit v2 on v1

v2 whole, which is shorter than its diff:
```python
import functools
import math

import jax
import jax.numpy as jnp
import numpy as np
from jax import lax
from jax.experimental import pallas as pl
from jax.experimental.pallas import tpu as pltpu
from jax.sharding import PartitionSpec as P

ITERS = 2
STEPS = 2 * ITERS
CHAINS = 4
NY, NX, NC = 4, 4, 2
NT = NY * NX * NC
NF = 8
GROUP = NX * NC
SLOTS = 64
PACK = 2
PS = SLOTS // PACK
GP = GROUP * PS
GS = GROUP * SLOTS
POS = 512
POINTS = 128
PC = 8
ROWS = 2 * POINTS // CHAINS
CHUNK = 2 * PC
PCS = ROWS // CHUNK
CUTS = NF // PCS
WIDE = POS // CUTS
ALL = NF * CHUNK
TIMES = 4 * NF
MESH = pl.DeviceIdType.MESH
BF = jnp.bfloat16
F32 = jnp.float32
Y_ORDER = (2, 1, 3, 0)
X_ORDER = (2, 1, 3, 0)
Z_ORDER = (4, 3, 5, 2, 6, 1, 7)
ORDER = (
    ("S1", 0, 0), ("W", 2, 1), ("S1", 1, 0), ("W", 3, 1), ("U", 0, 0), ("S2", 0, 0), ("S1", 2, 0), ("C", 0, 0),
    ("S2", 1, 0), ("S1", 3, 0), ("UT", 0, 0), ("OUT", 0, 0), ("W", 0, 0), ("S2", 2, 0), ("W", 1, 0), ("S2", 3, 0),
)


def dot(a, b):
    return jnp.dot(a, b, preferred_element_type=F32)


def dot_nt(a, b):
    return lax.dot_general(a, b, (((1,), (1,)), ((), ())), preferred_element_type=F32)


def phase_rows():
    times = np.arange(TIMES, dtype=np.float64)
    omegas = (np.arange(NF, dtype=np.float64) + 1.0) * (2.0 * math.pi / TIMES)
    phase = omegas[:, None] * times[None, :]
    both = np.stack([np.cos(phase), -np.sin(phase)], 1)
    return np.repeat(both.reshape(2 * NF, TIMES), PC, axis=0).astype(np.float32)


def combine(first, second, sign):
    first = first.reshape(PCS, 2, PC, first.shape[-1])
    second = second.reshape(PCS, 2, PC, second.shape[-1]) * sign
    real = first[:, 0] - second[:, 1]
    imag = first[:, 1] + second[:, 0]
    return jnp.stack([real, imag], 1).reshape(ROWS, first.shape[-1])


def to_chunks(field):
    parts = [field[:, i * WIDE : (i + 1) * WIDE].reshape(PCS, CHUNK, WIDE) for i in range(CUTS)]
    return jnp.stack(parts, 1).reshape(NF, CHUNK, WIDE)


def from_chunks(chunks):
    chunks = chunks.reshape(PCS, CUTS, CHUNK, WIDE)
    return jnp.concatenate([chunks[:, i].reshape(ROWS, WIDE) for i in range(CUTS)], 1)


def kernel(
    onset_rec, onset_src, ranks_hbm, phases_hbm, phases_t_hbm, start_hbm, u_hbm, v_hbm, fields_out,
    nat, tr, start, st, w_send, w_recv, z1_send, z1_recv, z2_send, z2_recv, mask, window, phases, phases_t, ranks,
    small_sem, out_sem, load_sem, ws_sem, wr_sem, z1s_sem, z1r_sem, z2s_sem, z2r_sem,
):
    f = lax.axis_index("freq")
    me = lax.axis_index("tile")
    y, x, c = me // GROUP, (me // NC) % NX, me % NC

    def tile_of(dy, dx, dc):
        return ((y + dy) % NY) * GROUP + ((x + dx) % NX) * NC + (c + dc) % NC

    small = [
        pltpu.make_async_copy(source, target, small_sem.at[i])
        for i, (source, target) in enumerate(
            ((start_hbm, start), (ranks_hbm, ranks), (phases_hbm, phases), (phases_t_hbm, phases_t))
        )
    ]

    def load(which, group, part):
        source = (u_hbm, v_hbm)[which]
        slots = source.at[:, group, :, pl.ds(part * PS, PS)]
        return pltpu.make_async_copy(slots, nat.at[which, :, group, part], load_sem.at[which, group, part])

    def loads(which):
        return [load(which, (y + dy) % NY, part) for dy in Y_ORDER for part in range(PACK)]

    def tiles(which, part, group):
        return nat[which, part, group].reshape(GS, POS)

    small[0].start()
    small[1].start()
    for copy in loads(1):
        copy.start()
    barrier = pltpu.get_barrier_semaphore()
    for dy in range(NY):
        for dx in range(NX):
            for dc in range(NC):
                if (dy, dx, dc) != (0, 0, 0):
                    pl.semaphore_signal(barrier, inc=1, device_id=(f, tile_of(dy, dx, dc)), device_id_type=MESH)
    for dz in range(1, NF):
        pl.semaphore_signal(barrier, inc=1, device_id=((f + dz) % NF, me), device_id_type=MESH)
    small[2].start()
    small[3].start()
    small[0].wait()

    for part in range(2):
        turned = start[part].T.reshape(CHAINS, PCS, PC, POS)
        for h in range(CHAINS):
            for k in range(PCS):
                r0 = k * CHUNK + part * PC
                st[h, r0 : r0 + PC, :] = turned[h, k]
    for h in range(CHAINS):
        z2_recv[0, h] = jnp.zeros((NF, CHUNK, WIDE), BF)

    small[1].wait()
    lanes = lax.broadcasted_iota(jnp.int32, (1, 128), 1)
    across = 128 // PS
    for adj in range(2):
        for group in range(NY):
            for quad in range(GROUP // across):
                rank = None
                for i in range(across):
                    tile = group * GROUP + quad * across + i
                    one = ranks[tile, me] if adj == 0 else ranks[me, tile]
                    rank = one if rank is None else jnp.where(lanes < i * PS, rank, one)
                for part in range(PACK):
                    l0 = part * GP + quad * 128
                    slot = lanes % PS + part * PS
                    mask[adj, group, :, l0 : l0 + 128] = jnp.where(slot < rank, 1.0, 0.0).astype(F32)

    def wait_u():
        for copy in loads(0):
            copy.wait()

    def turn_u():
        for group in range(NY):
            for part in range(2):
                tr[1, part, group] = tiles(0, part, group).T

    def make_windows():
        small[2].wait()
        small[3].wait()
        for adj, onset in ((0, onset_rec), (1, onset_src)):
            ticks = lax.broadcasted_iota(jnp.int32, (1, TIMES), 1)
            kept = jnp.where(ticks < onset[0], 1.0, 0.0).astype(F32)
            full = jnp.dot(phases[...] * kept, phases_t[...], precision=lax.Precision.HIGHEST, preferred_element_type=F32)
            r = lax.broadcasted_iota(jnp.int32, (ALL, ALL), 0)
            q = lax.broadcasted_iota(jnp.int32, (ALL, ALL), 1)
            full = jnp.where(r % PC == q % PC, full, 0.0)
            high = full.astype(BF)
            rest = full - high.astype(F32)
            middle = rest.astype(BF)
            low = (rest - middle.astype(F32)).astype(BF)
            window[adj, 0] = high
            window[adj, 1] = middle
            window[adj, 2] = low

    def send_group(t, h, dy, w):
        group = (y + dy) % NY
        w = jnp.concatenate([w[:, i * GP : (i + 1) * GP] for i in range(PACK)], 0).T
        w_send[t, h, pl.ds(group * GP, GP)] = w
        for dx in X_ORDER:
            for dc in (1, 0):
                to = group * GROUP + ((x + dx) % NX) * NC + (c + dc) % NC
                theirs, mine = pl.ds(to * PS, PS), pl.ds(me * PS, PS)
                if (dy, dx, dc) == (0, 0, 0):
                    w_recv[t, h, mine] = w_send[t, h, mine]
                    continue
                pltpu.make_async_remote_copy(
                    src_ref=w_send.at[t, h, theirs], dst_ref=w_recv.at[t, h, mine],
                    send_sem=ws_sem.at[t, h], recv_sem=wr_sem.at[t, h, dy],
                    device_id=(f, to), device_id_type=MESH,
                ).start()

    def first_coefficients(h):
        field = st[h].astype(BF)
        for dy in Y_ORDER:
            group = (y + dy) % NY
            for part in range(PACK):
                load(1, group, part).wait()
            w = combine(dot_nt(field, tiles(1, 0, group)), dot_nt(field, tiles(1, 1, group)), 1.0)
            send_group(0, h, dy, (w * mask[0, group]).astype(BF))

    def coefficients(t, h):
        adj = t % 2
        sign = (1 - 2 * adj).astype(F32)
        even = (1 - adj).astype(F32)

        @pl.when(t > 0)
        def _():
            z_wait(z2_recv.at[t, h], z2r_sem.at[t - 1, h])

        field = (st[h] * even + from_chunks(z2_recv[t, h]).astype(F32)).astype(BF)
        for dy in Y_ORDER:
            group = (y + dy) % NY
            w = combine(dot(field, tr[adj, 0, group]), dot(field, tr[adj, 1, group]), sign)
            send_group(t, h, dy, (w * mask[adj, group]).astype(BF))

        @pl.when(t > 0)
        def _():
            drain(t - 1, h)

    def w_wait(buffer, semaphore, count):
        part = buffer.at[pl.ds(0, count * PS)]
        pltpu.make_async_copy(part, part, semaphore).wait()

    def z_wait(buffer, semaphore):
        part = buffer.at[pl.ds(0, NF - 1)]
        pltpu.make_async_copy(part, part, semaphore).wait()

    def drain(t, h):
        w_wait(w_send.at[t, h], ws_sem.at[t, h], NT - 1)
        z_wait(z1_send.at[t, h], z1s_sem.at[t, h])
        z_wait(z2_send.at[t, h], z2s_sem.at[t, h])

    def z_send(source, target, send_sem, recv_sem):
        for dz in Z_ORDER:
            to = (f + dz) % NF
            pltpu.make_async_remote_copy(
                src_ref=source.at[to], dst_ref=target.at[f], send_sem=send_sem, recv_sem=recv_sem,
                device_id=(to, me), device_id_type=MESH,
            ).start()

    def apply(t, h):
        adj = t % 2
        sign = (1 - 2 * adj).astype(F32)
        real = imag = None
        for dy in Y_ORDER:
            group = (y - dy + NY) % NY
            w_wait(w_recv.at[t, h], wr_sem.at[t, h, dy], GROUP - 1 if dy == 0 else GROUP)
            w = w_recv[t, h, pl.ds(group * GP, GP)].T
            w = jnp.concatenate([w[i * ROWS : (i + 1) * ROWS] for i in range(PACK)], 1)
            one, two = dot(w, tiles(adj, 0, group)), dot(w, tiles(adj, 1, group))
            real, imag = (one, two) if real is None else (real + one, imag + two)
        z1_send[t, h] = to_chunks(combine(real, imag, sign).astype(BF))
        z1_recv[t, h, f] = z1_send[t, h, f]
        z_send(z1_send.at[t, h], z1_recv.at[t, h], z1s_sem.at[t, h], z1r_sem.at[t, h])

    def windowed(t, h):
        adj = t % 2
        z_wait(z1_recv.at[t, h], z1r_sem.at[t, h])
        traces = z1_recv[t, h].reshape(ALL, WIDE)
        out = dot(window[adj, 2], traces) + dot(window[adj, 1], traces) + dot(window[adj, 0], traces)
        z2_send[t, h] = out.astype(BF).reshape(NF, CHUNK, WIDE)
        z2_recv[t + 1, h, f] = z2_send[t, h, f]
        z_send(z2_send.at[t, h], z2_recv.at[t + 1, h], z2s_sem.at[t, h], z2r_sem.at[t, h])

    def hand_out(which):
        return pltpu.make_async_copy(z2_recv.at[STEPS - 1 + which], fields_out.at[which], out_sem.at[which])

    pl.semaphore_wait(barrier, NT - 1 + NF - 1)
    first_coefficients(0)
    for copy in loads(0):
        copy.start()
    for group in range(NY):
        for part in range(2):
            tr[0, part, group] = tiles(1, part, group).T

    def body(t, carry):
        for stage, h, behind in ORDER:
            if stage == "S1" and h == 0:
                pl.when(t > 0)(lambda: coefficients(t, 0))
            elif stage == "S1":
                coefficients(t, h)
            elif stage == "S2":
                apply(t, h)
            elif stage == "W" and behind:
                pl.when(t > 0)(lambda h=h: windowed(t - 1, h))
            elif stage == "W":
                windowed(t, h)
            elif stage == "OUT":
                pl.when(t == STEPS - 1)(lambda: hand_out(0).start())
            else:
                pl.when(t == 0)({"U": wait_u, "C": make_windows, "UT": turn_u}[stage])
        return carry

    lax.fori_loop(0, STEPS, body, 0)
    for stage, h, behind in ORDER:
        if stage == "W" and behind:
            windowed(jnp.int32(STEPS - 1), h)
    for h in range(CHAINS):
        drain(STEPS - 1, h)
    for h in range(CHAINS):
        z_wait(z2_recv.at[STEPS, h], z2r_sem.at[STEPS - 1, h])
    hand_out(1).start()
    hand_out(0).wait()
    hand_out(1).wait()


def finish_kernel(start, fields, plus_out, minus_out):
    for part in range(2):
        for which, out in enumerate((minus_out, plus_out)):
            rows = [
                from_chunks(fields[which, h]).astype(F32).reshape(PCS, 2, PC, POS)[:, part].reshape(ROWS // 2, POS)
                for h in range(CHAINS)
            ]
            values = jnp.concatenate(rows, 0).T
            out[part] = start[part] + values if which else values


def on_device(start_field, u_tiles, v_tiles, ranks, onset_rec, onset_src):
    rows = phase_rows()
    smem = pl.BlockSpec(memory_space=pltpu.SMEM)
    vmem = pl.BlockSpec(memory_space=pltpu.VMEM)
    hbm = pl.BlockSpec(memory_space=pl.ANY)
    field = jax.ShapeDtypeStruct((2, POS, POINTS), F32)
    start_field = start_field.reshape(2, POS, POINTS)
    fields = pl.pallas_call(
        kernel,
        out_shape=jax.ShapeDtypeStruct((2, CHAINS, NF, CHUNK, WIDE), BF),
        in_specs=[smem, smem, hbm, hbm, hbm, hbm, hbm, hbm],
        out_specs=hbm,
        scratch_shapes=[
            pltpu.VMEM((2, 2, NY, PACK, GROUP, PS, POS), BF),
            pltpu.VMEM((2, 2, NY, POS, GS), BF),
            pltpu.VMEM((2, POS, POINTS), F32),
            pltpu.VMEM((CHAINS, ROWS, POS), F32),
            pltpu.VMEM((STEPS, CHAINS, NT * PS, PACK * ROWS), BF),
            pltpu.VMEM((STEPS, CHAINS, NT * PS, PACK * ROWS), BF),
            pltpu.VMEM((STEPS, CHAINS, NF, CHUNK, WIDE), BF),
            pltpu.VMEM((STEPS, CHAINS, NF, CHUNK, WIDE), BF),
            pltpu.VMEM((STEPS, CHAINS, NF, CHUNK, WIDE), BF),
            pltpu.VMEM((STEPS + 1, CHAINS, NF, CHUNK, WIDE), BF),
            pltpu.VMEM((2, NY, 1, GS), F32),
            pltpu.VMEM((2, 3, ALL, ALL), BF),
            pltpu.VMEM((ALL, TIMES), F32),
            pltpu.VMEM((TIMES, ALL), F32),
            pltpu.SMEM((NT, NT), jnp.int32),
            pltpu.SemaphoreType.DMA((4,)),
            pltpu.SemaphoreType.DMA((2,)),
            pltpu.SemaphoreType.DMA((2, NY, PACK)),
            pltpu.SemaphoreType.DMA((STEPS, CHAINS)),
            pltpu.SemaphoreType.DMA((STEPS, CHAINS, NY)),
            pltpu.SemaphoreType.DMA((STEPS, CHAINS)),
            pltpu.SemaphoreType.DMA((STEPS, CHAINS)),
            pltpu.SemaphoreType.DMA((STEPS, CHAINS)),
            pltpu.SemaphoreType.DMA((STEPS, CHAINS)),
        ],
        compiler_params=pltpu.CompilerParams(
            collective_id=0, has_side_effects=True, vmem_limit_bytes=63 * 2**20
        ),
        name="marchenko",
    )(
        onset_rec,
        onset_src,
        ranks.reshape(NT, NT),
        jnp.asarray(rows),
        jnp.asarray(2.0 / TIMES * rows.T),
        start_field,
        u_tiles.reshape(2, NY, GROUP, SLOTS, POS),
        v_tiles.reshape(2, NY, GROUP, SLOTS, POS),
    )
    plus, minus = pl.pallas_call(
        finish_kernel,
        out_shape=(field, field),
        in_specs=[vmem, vmem],
        out_specs=(vmem, vmem),
        name="finish",
    )(start_field, fields)
    shape = (2, 1, POS, POINTS)
    return plus.reshape(shape), minus.reshape(shape)


def solution(mesh):
    in_specs = (
        P(None, "freq", "tile", None),
        P(None, "freq", "tile", None, None, None),
        P(None, "freq", None, "tile", None, None),
        P("freq", None, None),
        P("tile"),
        P("tile"),
    )
    out_specs = (P(None, "freq", "tile", None), P(None, "freq", "tile", None))
    return jax.shard_map(
        on_device, mesh=mesh, in_specs=in_specs, out_specs=out_specs, check_vma=False
    )
```

time: 114 us -> 97.4 us (0.85)
  Pallas kernels: 107 us -> 94.5 us
  local copies, waits for them, and re-layouts: 4.9 us -> 0 us
    pallas_call x1 -> x2, Pallas kernels: 107 us -> 94.5 us  [the longest x1 92.1 us: on_device(): pl.pallas_call(kernel, out_shape=jax.ShapeDtypeStruct((2, CHAINS, NF, CHU...]
    unnamed x10 -> x0, local copies, waits for them, and re-layouts: 4.9 us -> none
where the time goes in v2:
time: 97.4 us; the launch traced here: 96.4 us
  Pallas kernels  94.5 us (97%)
  between operations  1.93 us (2%)
    pallas_call x1, Pallas kernels, on_device(): pl.pallas_call(kernel, out_shape=jax.ShapeDtypeStruct((2, CHAINS, NF, CHU...  92.1 us
    pallas_call x1, Pallas kernels, on_device(): pl.pallas_call(finish_kernel, out_shape=(field, field), in_specs=[vmem, v...  2.34 us

profile of v2, /device:TPU:8, one launch (start us, length us, event | category | flops | bytes accessed | tf_op | source)
XLA Modules:
  0.0 96.4 jit_solution(1900871464165392693)
XLA Ops:
  1.9 92.1 %marchenko.1.fields = bf16[2,4,8,16,256]{4,3,2,1,0:T(8,128)(2,1)} custom-call(s32[1]{0:T(128)S(6)} %copy.12.onset_rec, s32[1]{0:T(128)S(6)} %copy.13.onset_src, s32[32,32]{1,0:T(8,128)} %bitcast.14, f32[128,32]{1,0:T(8,128)} %constant.4.clone.phases_hbm, f32[32,128]{1,0:T(8,128)} %constant.5.clone.phases_t_hbm, f32[2,512,128]{2,1,0:T(8,128)} %bitcast.12, ...), custom_call_target="tpu_custom_call" | custom-call | tf_op jit(solution)/shard_map/marchenko/pallas_call | solution.py:328
  94.1 2.3 %finish.1 = (f32[2,512,128]{2,1,0:T(8,128)}, f32[2,512,128]{2,1,0:T(8,128)}) custom-call(f32[2,512,128]{2,1,0:T(8,128)} %bitcast.13, bf16[2,4,8,16,256]{4,3,2,1,0:T(8,128)(2,1)} %marchenko.1.fields), custom_call_target="tpu_custom_call" | custom-call | tf_op jit(solution)/shard_map/finish/pallas_call | solution.py:373

commit v3 on v2

--- a/solution.py
+++ b/solution.py
@@ -38,8 +38,8 @@
 X_ORDER = (2, 1, 3, 0)
 Z_ORDER = (4, 3, 5, 2, 6, 1, 7)
 ORDER = (
-    ("S1", 0, 0), ("W", 2, 1), ("S1", 1, 0), ("W", 3, 1), ("U", 0, 0), ("S2", 0, 0), ("S1", 2, 0), ("C", 0, 0),
-    ("S2", 1, 0), ("S1", 3, 0), ("UT", 0, 0), ("OUT", 0, 0), ("W", 0, 0), ("S2", 2, 0), ("W", 1, 0), ("S2", 3, 0),
+    ("S1", 0, 0), ("S2", 3, 1), ("W", 2, 1), ("S1", 1, 0), ("U", 0, 0), ("S2", 0, 0), ("W", 3, 1), ("C", 0, 0),
+    ("S1", 2, 0), ("S2", 1, 0), ("UT", 0, 0), ("W", 0, 0), ("S1", 3, 0), ("OUT", 0, 0), ("S2", 2, 0), ("W", 1, 0),
 )
 
 
@@ -282,6 +282,8 @@
                 pl.when(t > 0)(lambda: coefficients(t, 0))
             elif stage == "S1":
                 coefficients(t, h)
+            elif stage == "S2" and behind:
+                pl.when(t > 0)(lambda h=h: apply(t - 1, h))
             elif stage == "S2":
                 apply(t, h)
             elif stage == "W" and behind:
@@ -296,8 +298,8 @@
 
     lax.fori_loop(0, STEPS, body, 0)
     for stage, h, behind in ORDER:
-        if stage == "W" and behind:
-            windowed(jnp.int32(STEPS - 1), h)
+        if behind:
+            (apply if stage == "S2" else windowed)(jnp.int32(STEPS - 1), h)
     for h in range(CHAINS):
         drain(STEPS - 1, h)
     for h in range(CHAINS):
@@ -311,7 +313,7 @@
     for part in range(2):
         for which, out in enumerate((minus_out, plus_out)):
             rows = [
-                from_chunks(fields[which, h]).astype(F32).reshape(PCS, 2, PC, POS)[:, part].reshape(ROWS // 2, POS)
+                fields[which, h].reshape(ROWS, WIDE).astype(F32).reshape(PCS, 2, PC, WIDE)[:, part].reshape(ROWS // 2, WIDE)
                 for h in range(CHAINS)
             ]
             values = jnp.concatenate(rows, 0).T
@@ -370,13 +372,15 @@
         u_tiles.reshape(2, NY, GROUP, SLOTS, POS),
         v_tiles.reshape(2, NY, GROUP, SLOTS, POS),
     )
+    cut = pl.BlockSpec((2, WIDE, POINTS), lambda i: (0, i, 0))
     plus, minus = pl.pallas_call(
         finish_kernel,
         out_shape=(field, field),
-        in_specs=[vmem, vmem],
-        out_specs=(vmem, vmem),
+        grid=(CUTS,),
+        in_specs=[cut, pl.BlockSpec((2, CHAINS, PCS, None, CHUNK, WIDE), lambda i: (0, 0, 0, i, 0, 0))],
+        out_specs=(cut, cut),
         name="finish",
-    )(start_field, fields)
+    )(start_field, fields.reshape(2, CHAINS, PCS, CUTS, CHUNK, WIDE))
     shape = (2, 1, POS, POINTS)
     return plus.reshape(shape), minus.reshape(shape)
 

time: 97.4 us -> 93.6 us (0.961)
  Pallas kernels: 94.5 us -> 91.2 us
    pallas_call x1, Pallas kernels: 92.1 us -> 89 us  [on_device(): pl.pallas_call(kernel, out_shape=jax.ShapeDtypeStruct((2, CHAINS, NF, CHU...]
where the time goes in v3:
time: 93.6 us; the launch traced here: 93.1 us
  Pallas kernels  91.2 us (97%)
  between operations  1.93 us (2%)
    pallas_call x1, Pallas kernels, on_device(): pl.pallas_call(kernel, out_shape=jax.ShapeDtypeStruct((2, CHAINS, NF, CHU...  89 us
    pallas_call x1, Pallas kernels, on_device(): pl.pallas_call(finish_kernel, out_shape=(field, field), grid=(CUTS,), in_...  2.15 us

profile of v3, /device:TPU:8, one launch (start us, length us, event | category | flops | bytes accessed | tf_op | source)
XLA Modules:
  0.0 93.1 jit_solution(8105237065205068305)
XLA Ops:
  1.9 89.0 %marchenko.1 = bf16[2,4,8,16,256]{4,3,2,1,0:T(8,128)(2,1)} custom-call(s32[1]{0:T(128)S(6)} %copy.12.onset_rec, s32[1]{0:T(128)S(6)} %copy.13.onset_src, s32[32,32]{1,0:T(8,128)} %bitcast.16, f32[128,32]{1,0:T(8,128)} %constant.4.clone.phases_hbm, f32[32,128]{1,0:T(8,128)} %constant.5.clone.phases_t_hbm, f32[2,512,128]{2,1,0:T(8,128)} %bitcast.13, ...), custom_call_target="tpu_custom_call" | custom-call | tf_op jit(solution)/shard_map/marchenko/pallas_call | solution.py:330
  91.0 2.2 %finish.1 = (f32[2,512,128]{2,1,0:T(8,128)}, f32[2,512,128]{2,1,0:T(8,128)}) custom-call(f32[2,512,128]{2,1,0:T(8,128)} %bitcast.14, bf16[2,4,4,2,16,256]{5,4,3,2,1,0:T(8,128)(2,1)} %bitcast.15), custom_call_target="tpu_custom_call" | custom-call | tf_op jit(solution)/shard_map/finish/pallas_call | solution.py:376

commit v4 on v3

--- a/solution.py
+++ b/solution.py
@@ -35,6 +35,7 @@
 BF = jnp.bfloat16
 F32 = jnp.float32
 Y_ORDER = (2, 1, 3, 0)
+ARRIVAL = (0, 1, 3, 2)
 X_ORDER = (2, 1, 3, 0)
 Z_ORDER = (4, 3, 5, 2, 6, 1, 7)
 ORDER = (
@@ -245,7 +246,7 @@
         adj = t % 2
         sign = (1 - 2 * adj).astype(F32)
         real = imag = None
-        for dy in Y_ORDER:
+        for dy in ARRIVAL:
             group = (y - dy + NY) % NY
             w_wait(w_recv.at[t, h], wr_sem.at[t, h, dy], GROUP - 1 if dy == 0 else GROUP)
             w = w_recv[t, h, pl.ds(group * GP, GP)].T
@@ -265,8 +266,13 @@
         z2_recv[t + 1, h, f] = z2_send[t, h, f]
         z_send(z2_send.at[t, h], z2_recv.at[t + 1, h], z2s_sem.at[t, h], z2r_sem.at[t, h])
 
-    def hand_out(which):
-        return pltpu.make_async_copy(z2_recv.at[STEPS - 1 + which], fields_out.at[which], out_sem.at[which])
+    def hand_out(which, h):
+        source, target = z2_recv.at[STEPS - 1 + which, h], fields_out.at[which, h]
+        return pltpu.make_async_copy(source, target, out_sem.at[which, h])
+
+    def hand_out_first():
+        for h in range(CHAINS):
+            hand_out(0, h).start()
 
     pl.semaphore_wait(barrier, NT - 1 + NF - 1)
     first_coefficients(0)
@@ -291,7 +297,7 @@
             elif stage == "W":
                 windowed(t, h)
             elif stage == "OUT":
-                pl.when(t == STEPS - 1)(lambda: hand_out(0).start())
+                pl.when(t == STEPS - 1)(hand_out_first)
             else:
                 pl.when(t == 0)({"U": wait_u, "C": make_windows, "UT": turn_u}[stage])
         return carry
@@ -304,9 +310,10 @@
         drain(STEPS - 1, h)
     for h in range(CHAINS):
         z_wait(z2_recv.at[STEPS, h], z2r_sem.at[STEPS - 1, h])
-    hand_out(1).start()
-    hand_out(0).wait()
-    hand_out(1).wait()
+        hand_out(1, h).start()
+    for which in range(2):
+        for h in range(CHAINS):
+            hand_out(which, h).wait()
 
 
 def finish_kernel(start, fields, plus_out, minus_out):
@@ -349,7 +356,7 @@
             pltpu.VMEM((TIMES, ALL), F32),
             pltpu.SMEM((NT, NT), jnp.int32),
             pltpu.SemaphoreType.DMA((4,)),
-            pltpu.SemaphoreType.DMA((2,)),
+            pltpu.SemaphoreType.DMA((2, CHAINS)),
             pltpu.SemaphoreType.DMA((2, NY, PACK)),
             pltpu.SemaphoreType.DMA((STEPS, CHAINS)),
             pltpu.SemaphoreType.DMA((STEPS, CHAINS, NY)),

time: 93.6 us -> 93.7 us (level)
  no operation moved by 1% of the time
where the time goes in v4:
time: 93.7 us; the launch traced here: 93.6 us
  Pallas kernels  91.7 us (98%)
  between operations  1.93 us (2%)
    pallas_call x1, Pallas kernels, on_device(): pl.pallas_call(kernel, out_shape=jax.ShapeDtypeStruct((2, CHAINS, NF, CHU...  89.5 us
    pallas_call x1, Pallas kernels, on_device(): pl.pallas_call(finish_kernel, out_shape=(field, field), grid=(CUTS,), in_...  2.15 us

profile of v4, /device:TPU:8, one launch (start us, length us, event | category | flops | bytes accessed | tf_op | source)
XLA Modules:
  0.0 93.6 jit_solution(5756527468551063531)
XLA Ops:
  1.9 89.5 %marchenko.1 = bf16[2,4,8,16,256]{4,3,2,1,0:T(8,128)(2,1)} custom-call(s32[1]{0:T(128)S(6)} %copy.12.onset_rec, s32[1]{0:T(128)S(6)} %copy.13.onset_src, s32[32,32]{1,0:T(8,128)} %bitcast.16, f32[128,32]{1,0:T(8,128)} %constant.4.clone.phases_hbm, f32[32,128]{1,0:T(8,128)} %constant.5.clone.phases_t_hbm, f32[2,512,128]{2,1,0:T(8,128)} %bitcast.13, ...), custom_call_target="tpu_custom_call" | custom-call | tf_op jit(solution)/shard_map/marchenko/pallas_call | solution.py:337
  91.5 2.2 %finish.1 = (f32[2,512,128]{2,1,0:T(8,128)}, f32[2,512,128]{2,1,0:T(8,128)}) custom-call(f32[2,512,128]{2,1,0:T(8,128)} %bitcast.14, bf16[2,4,4,2,16,256]{5,4,3,2,1,0:T(8,128)(2,1)} %bitcast.15), custom_call_target="tpu_custom_call" | custom-call | tf_op jit(solution)/shard_map/finish/pallas_call | solution.py:383
